TPU v7x, 768 devices: a whole 4x8x12 slice. The times are simulated.
768 devices in a mesh: wide: 96 (over y_hi, z, core), narrow: 8 (over x, y_lo).
Axes of the slice: x: 4, y: 8 (y_hi: 4, y_lo: 2; y = y_hi * 2 + y_lo), z: 12, core: 2. Of those that a mesh axis runs over, the one named last changes fastest.
Arguments:
- embeddings: float32 [49152, 256], P(('wide', 'narrow')), may hold values from -1.5 to 1.5
- co_engagement: bfloat16 [49152, 4096], P('wide', 'narrow'), may hold values from -6 to 6
- confidence: bfloat16 [49152, 4096], P('wide', 'narrow'), may hold values from 0.099609375 to 1
- tile_offset: int32 [96, 8], P('wide', 'narrow'), may hold values from 0 to 7, each once within a row
Outputs:
- updated: float32 [49152, 256], P(('wide', 'narrow'))
Inputs may be any that keep to these rules, and one draw needn't show every extreme that they name: Each row of tile_offset names each of 0 to 7 once.
All inputs are finite; a program needn't handle non-finite values.
Results may differ from a plain program's by a relative error of at most 0.0003.
Values sent between devices are 32-bit elements; how exact they have to be, the bound alone decides.
A program may use at most 32 MiB of HBM per device.

v0:
```python
import math

import jax
import jax.numpy as jnp
from jax import lax
from jax.sharding import PartitionSpec as P

ITERS = 2


def passed_along(block, axis, distance):
    devices = range(lax.axis_size(axis))
    route = [((i - distance) % len(devices), i) for i in devices]
    return lax.ppermute(block, axis, route)


def body(embeddings, co_engagement, confidence, tile_offset):
    rows_dev, width = embeddings.shape
    lane_count = lax.axis_size("narrow")
    block_size = rows_dev * lane_count
    step_rate = 0.75 * math.sqrt(width) / (lane_count * block_size)
    all_dist = lax.all_gather(tile_offset[0], "narrow", axis=0, tiled=True) + 1
    inverse = jnp.argsort(all_dist)
    x_tile = co_engagement.astype(jnp.float32)
    w_tile = confidence.astype(jnp.float32)
    current = embeddings
    for step in range(ITERS):
        own = lax.all_gather(current, "narrow", axis=0, tiled=True)
        shifted = [passed_along(current, "wide", -dist) for dist in range(1, lane_count + 1)]
        pieces = jnp.stack(shifted)
        outgoing = jnp.take(pieces, all_dist - 1, axis=0)
        incoming = lax.all_to_all(outgoing, "narrow", split_axis=0, concat_axis=0, tiled=True)
        other = incoming.reshape(block_size, width)
        predicted = lax.dot_general(
            own,
            other,
            (((1,), (1,)), ((), ())),
            precision=lax.Precision.HIGHEST,
            preferred_element_type=jnp.float32,
        )
        weighted = w_tile * (x_tile - predicted)
        row_grad = -jnp.dot(
            weighted, other, precision=lax.Precision.HIGHEST, preferred_element_type=jnp.float32
        )
        back = -lax.dot_general(
            weighted,
            own,
            (((0,), (0,)), ((), ())),
            precision=lax.Precision.HIGHEST,
            preferred_element_type=jnp.float32,
        )
        mine = lax.psum_scatter(row_grad, "narrow", scatter_dimension=0, tiled=True)
        received = lax.all_to_all(
            back.reshape(lane_count, rows_dev, width),
            "narrow",
            split_axis=0,
            concat_axis=0,
            tiled=True,
        )
        by_dist = jnp.take(received, inverse, axis=0)
        for dist in range(1, lane_count + 1):
            mine = mine + passed_along(by_dist[dist - 1], "wide", dist)
        current = current - step_rate * mine
    return current


def solution(mesh):
    in_specs = (
        P(("wide", "narrow"), None),
        P("wide", "narrow"),
        P("wide", "narrow"),
        P("wide", "narrow"),
    )
    out_specs = P(("wide", "narrow"), None)
    return jax.shard_map(body, mesh=mesh, in_specs=in_specs, out_specs=out_specs, check_vma=False)
```

profile of v0, /device:TPU:16, one launch (start us, length us, event | category | flops | bytes accessed | tf_op | source)
XLA Modules:
  0.0 344.6 jit_solution(13500719784504000522)
XLA Ops:
  6.5 14.3 %collective-permute-start.7 = (f32[64,256]{1,0:T(8,128)}, f32[64,256]{1,0:T(8,128)S(1)}, u32[]{:S(2)}, u32[]{:S(2)}) collective-permute-start(f32[64,256]{1,0:T(8,128)} %param.6), channel_id=1, source_target_pairs={{64,0},{72,8},{80,16},{88,24},{96,32},{104,40},{112,48},{120,56},{... | collective-permute-start | bytes 196616 | tf_op jit(solution)/shard_map/ppermute | solution.py:14
  24.9 13.7 %collective-permute-start.4 = (f32[64,256]{1,0:T(8,128)}, f32[64,256]{1,0:T(8,128)S(1)}, u32[]{:S(2)}, u32[]{:S(2)}) collective-permute-start(f32[64,256]{1,0:T(8,128)} %param.6), channel_id=1, source_target_pairs={{40,0},{48,8},{56,16},{64,24},{72,32},{80,40},{88,48},{96,56},{104... | collective-permute-start | bytes 196616 | tf_op jit(solution)/shard_map/ppermute | solution.py:14
  43.2 11.7 %all-reduce = s32[8]{0:T(128)S(1)} all-reduce(s32[8]{0:T(128)S(1)} %bitcast_dynamic-update-slice_fusion.16), channel_id=2, replica_groups=mesh['wide'=96,'narrow'=8] {'narrow'}, use_global_device_ids=true, to_apply=%add | all-reduce | flops 8 | bytes 64 | tf_op jit(solution)/shard_map/all_gather | solution.py:22
  57.4 3.9 %collective-permute-done.1 = f32[64,256]{1,0:T(8,128)S(1)} collective-permute-done((f32[64,256]{1,0:T(8,128)}, f32[64,256]{1,0:T(8,128)S(1)}, u32[]{:S(2)}, u32[]{:S(2)}) %collective-permute-start.1) | collective-permute-done | bytes 65568 | tf_op jit(solution)/shard_map/ppermute | solution.py:14
  63.3 4.1 %collective-permute-done.2 = f32[64,256]{1,0:T(8,128)S(1)} collective-permute-done((f32[64,256]{1,0:T(8,128)S(1)}, f32[64,256]{1,0:T(8,128)S(1)}, u32[]{:S(2)}, u32[]{:S(2)}) %collective-permute-start.2) | collective-permute-done | bytes 65568 | tf_op jit(solution)/shard_map/ppermute | solution.py:14
  69.4 5.6 %collective-permute-done.3 = f32[64,256]{1,0:T(8,128)S(1)} collective-permute-done((f32[64,256]{1,0:T(8,128)S(1)}, f32[64,256]{1,0:T(8,128)S(1)}, u32[]{:S(2)}, u32[]{:S(2)}) %collective-permute-start.3) | collective-permute-done | bytes 65568 | tf_op jit(solution)/shard_map/ppermute | solution.py:14
  81.5 34.0 %all_gather.10 = f32[512,256]{1,0:T(8,128)S(1)} all-gather(f32[64,256]{1,0:T(8,128)S(1)} %copy-done.2), channel_id=1, replica_groups=mesh['wide'=96,'narrow'=8] {'narrow'}, dimensions={0}, use_global_device_ids=true | all-gather | bytes 589824 | tf_op jit(solution)/shard_map/all_gather | solution.py:28
  125.6 4.9 %all-to-all-done.1 = f32[8,64,256]{2,1,0:T(8,128)S(1)} async-done(((f32[8,64,256]{2,1,0:T(8,128)}), f32[8,64,256]{2,1,0:T(8,128)S(1)}, u32[]{:S(2)}, u32[]{:S(2)}) %all-to-all-start.1) | async-done | bytes 524320 | tf_op jit(solution)/shard_map/all_to_all | solution.py:53
  138.6 13.7 %collective-permute-start.13 = (f32[64,256]{1,0:T(8,128)S(1)}, f32[64,256]{1,0:T(8,128)S(1)}, u32[]{:S(2)}, u32[]{:S(2)}) collective-permute-start(f32[64,256]{1,0:T(8,128)S(1)} %get-tuple-element.19), channel_id=1, source_target_pairs={{720,0},{728,8},{736,16},{744,24},{752,32},{760,40},{0,48},{8,56},... | collective-permute-start | bytes 196616 | tf_op jit(solution)/shard_map/ppermute | solution.py:14
  160.9 3.9 %collective-permute-done.12 = f32[64,256]{1,0:T(8,128)S(1)} collective-permute-done((f32[64,256]{1,0:T(8,128)S(1)}, f32[64,256]{1,0:T(8,128)S(1)}, u32[]{:S(2)}, u32[]{:S(2)}) %collective-permute-start.12) | collective-permute-done | bytes 65568 | tf_op jit(solution)/shard_map/ppermute | solution.py:14
  172.5 10.2 %reduce-scatter.3.cloned.1.call-done = f32[64,256]{1,0:T(8,128)} async-done(((f32[512,256]{1,0:T(8,128)}), f32[64,256]{1,0:T(8,128)}) %reduce-scatter.3.cloned.1.call-update) | async-done | bytes 65552 | tf_op jit(solution)/shard_map/reduce_scatter | solution.py:52
  189.4 4.3 %collective-permute-start.21 = (f32[64,256]{1,0:T(8,128)S(1)}, f32[64,256]{1,0:T(8,128)S(1)}, u32[]{:S(2)}, u32[]{:S(2)}) collective-permute-start(f32[64,256]{1,0:T(8,128)S(1)} %multiply_subtract_fusion.1), channel_id=1, source_target_pairs={{48,0},{56,8},{64,16},{72,24},{80,32},{88,40},{96,48},{104,56},{11... | collective-permute-start | bytes 196616 | tf_op jit(solution)/shard_map/ppermute | solution.py:14
  193.7 5.5 %collective-permute-start.20 = (f32[64,256]{1,0:T(8,128)S(1)}, f32[64,256]{1,0:T(8,128)S(1)}, u32[]{:S(2)}, u32[]{:S(2)}) collective-permute-start(f32[64,256]{1,0:T(8,128)S(1)} %multiply_subtract_fusion.1), channel_id=1, source_target_pairs={{40,0},{48,8},{56,16},{64,24},{72,32},{80,40},{88,48},{96,56},{104... | collective-permute-start | bytes 196616 | tf_op jit(solution)/shard_map/ppermute | solution.py:14
  199.2 4.7 %collective-permute-start.17 = (f32[64,256]{1,0:T(8,128)S(1)}, f32[64,256]{1,0:T(8,128)S(1)}, u32[]{:S(2)}, u32[]{:S(2)}) collective-permute-start(f32[64,256]{1,0:T(8,128)S(1)} %multiply_subtract_fusion.1), channel_id=1, source_target_pairs={{16,0},{24,8},{32,16},{40,24},{48,32},{56,40},{64,48},{72,56},{80,... | collective-permute-start | bytes 196616 | tf_op jit(solution)/shard_map/ppermute | solution.py:14
  204.0 4.5 %collective-permute-done.17 = f32[64,256]{1,0:T(8,128)S(1)} collective-permute-done((f32[64,256]{1,0:T(8,128)S(1)}, f32[64,256]{1,0:T(8,128)S(1)}, u32[]{:S(2)}, u32[]{:S(2)}) %collective-permute-start.17) | collective-permute-done | bytes 65568 | tf_op jit(solution)/shard_map/ppermute | solution.py:14
  214.4 4.5 %collective-permute-start.19 = (f32[64,256]{1,0:T(8,128)S(1)}, f32[64,256]{1,0:T(8,128)S(1)}, u32[]{:S(2)}, u32[]{:S(2)}) collective-permute-start(f32[64,256]{1,0:T(8,128)S(1)} %multiply_subtract_fusion.1), channel_id=1, source_target_pairs={{32,0},{40,8},{48,16},{56,24},{64,32},{72,40},{80,48},{88,56},{96,... | collective-permute-start | bytes 196616 | tf_op jit(solution)/shard_map/ppermute | solution.py:14
  223.1 6.3 %all-to-all-start.2 = ((f32[8,64,256]{2,1,0:T(8,128)}), f32[8,64,256]{2,1,0:T(8,128)S(1)}, u32[]{:S(2)}, u32[]{:S(2)}) async-start(f32[8,64,256]{2,1,0:T(8,128)} %broadcast_select_fusion.1), calls=%async_computation.3 | async-start | bytes 1048576 | tf_op jit(solution)/shard_map/all_to_all | solution.py:32
  229.3 35.3 %all_gather.11 = f32[512,256]{1,0:T(8,128)S(1)} all-gather(f32[64,256]{1,0:T(8,128)S(1)} %multiply_subtract_fusion.1), channel_id=1, replica_groups=mesh['wide'=96,'narrow'=8] {'narrow'}, dimensions={0}, use_global_device_ids=true | all-gather | bytes 589824 | tf_op jit(solution)/shard_map/all_gather | solution.py:28
  274.0 5.7 %all-to-all-done.3 = f32[8,64,256]{2,1,0:T(8,128)S(1)} async-done(((f32[8,64,256]{2,1,0:T(8,128)}), f32[8,64,256]{2,1,0:T(8,128)S(1)}, u32[]{:S(2)}, u32[]{:S(2)}) %all-to-all-start.3) | async-done | bytes 524320 | tf_op jit(solution)/shard_map/all_to_all | solution.py:53
  282.4 4.1 %collective-permute-start.31 = (f32[64,256]{1,0:T(8,128)S(1)}, f32[64,256]{1,0:T(8,128)S(1)}, u32[]{:S(2)}, u32[]{:S(2)}) collective-permute-start(f32[64,256]{1,0:T(8,128)S(1)} %get-tuple-element.9), channel_id=1, source_target_pairs={{704,0},{712,8},{720,16},{728,24},{736,32},{744,40},{752,48},{760,... | collective-permute-start | bytes 196616 | tf_op jit(solution)/shard_map/ppermute | solution.py:14
  286.6 4.7 %collective-permute-start.30 = (f32[64,256]{1,0:T(8,128)S(1)}, f32[64,256]{1,0:T(8,128)S(1)}, u32[]{:S(2)}, u32[]{:S(2)}) collective-permute-start(f32[64,256]{1,0:T(8,128)S(1)} %get-tuple-element.10), channel_id=1, source_target_pairs={{712,0},{720,8},{728,16},{736,24},{744,32},{752,40},{760,48},{0,56... | collective-permute-start | bytes 196616 | tf_op jit(solution)/shard_map/ppermute | solution.py:14
  291.3 15.0 %collective-permute-start.29 = (f32[64,256]{1,0:T(8,128)S(1)}, f32[64,256]{1,0:T(8,128)S(1)}, u32[]{:S(2)}, u32[]{:S(2)}) collective-permute-start(f32[64,256]{1,0:T(8,128)S(1)} %get-tuple-element.11), channel_id=1, source_target_pairs={{720,0},{728,8},{736,16},{744,24},{752,32},{760,40},{0,48},{8,56},... | collective-permute-start | bytes 196616 | tf_op jit(solution)/shard_map/ppermute | solution.py:14
  322.1 3.7 %collective-permute-done.25 = f32[64,256]{1,0:T(8,128)S(1)} collective-permute-done((f32[64,256]{1,0:T(8,128)S(1)}, f32[64,256]{1,0:T(8,128)S(1)}, u32[]{:S(2)}, u32[]{:S(2)}) %collective-permute-start.25) | collective-permute-done | bytes 65568 | tf_op jit(solution)/shard_map/ppermute | solution.py:14
  325.8 10.5 %reduce-scatter.5.cloned.1.call-done = f32[64,256]{1,0:T(8,128)} async-done(((f32[512,256]{1,0:T(8,128)}), f32[64,256]{1,0:T(8,128)}) %reduce-scatter.5.cloned.1.call-update) | async-done | bytes 65552 | tf_op jit(solution)/shard_map/reduce_scatter | solution.py:52
  (110 shorter events, 100.8 us)
Async XLA Ops:
  6.5 68.5 %collective-permute-start.7 = (f32[64,256]{1,0:T(8,128)}, f32[64,256]{1,0:T(8,128)S(1)}, u32[]{:S(2)}, u32[]{:S(2)}) collective-permute-start(f32[64,256]{1,0:T(8,128)} %param.6), channel_id=1, source_target_pairs={{64,0},{72,8},{80,16},{88,24},{96,32},{104,40},{112,48},{120,56},{... | collective-permute-start | bytes 196616 | tf_op jit(solution)/shard_map/ppermute | solution.py:14
  20.9 54.2 %collective-permute-start.6 = (f32[64,256]{1,0:T(8,128)}, f32[64,256]{1,0:T(8,128)S(1)}, u32[]{:S(2)}, u32[]{:S(2)}) collective-permute-start(f32[64,256]{1,0:T(8,128)} %param.6), channel_id=1, source_target_pairs={{56,0},{64,8},{72,16},{80,24},{88,32},{96,40},{104,48},{112,56},{1... | collective-permute-start | bytes 196616 | tf_op jit(solution)/shard_map/ppermute | solution.py:14
  22.8 52.2 %collective-permute-start.5 = (f32[64,256]{1,0:T(8,128)}, f32[64,256]{1,0:T(8,128)S(1)}, u32[]{:S(2)}, u32[]{:S(2)}) collective-permute-start(f32[64,256]{1,0:T(8,128)} %param.6), channel_id=1, source_target_pairs={{48,0},{56,8},{64,16},{72,24},{80,32},{88,40},{96,48},{104,56},{11... | collective-permute-start | bytes 196616 | tf_op jit(solution)/shard_map/ppermute | solution.py:14
  24.9 50.0 %collective-permute-start.4 = (f32[64,256]{1,0:T(8,128)}, f32[64,256]{1,0:T(8,128)S(1)}, u32[]{:S(2)}, u32[]{:S(2)}) collective-permute-start(f32[64,256]{1,0:T(8,128)} %param.6), channel_id=1, source_target_pairs={{40,0},{48,8},{56,16},{64,24},{72,32},{80,40},{88,48},{96,56},{104... | collective-permute-start | bytes 196616 | tf_op jit(solution)/shard_map/ppermute | solution.py:14
  41.3 13.7 %collective-permute-start = (f32[64,256]{1,0:T(8,128)}, f32[64,256]{1,0:T(8,128)S(1)}, u32[]{:S(2)}, u32[]{:S(2)}) collective-permute-start(f32[64,256]{1,0:T(8,128)} %param.6), channel_id=1, source_target_pairs={{8,0},{16,8},{24,16},{32,24},{40,32},{48,40},{56,48},{64,56},{72,6... | collective-permute-start | bytes 196616 | tf_op jit(solution)/shard_map/ppermute | solution.py:14
  76.6 38.9 %all-to-all-start = ((f32[8,64,256]{2,1,0:T(8,128)}), f32[8,64,256]{2,1,0:T(8,128)S(1)}, u32[]{:S(2)}, u32[]{:S(2)}) async-start(f32[8,64,256]{2,1,0:T(8,128)} %broadcast_select_fusion.3), calls=%async_computation | async-start | bytes 1048576 | tf_op jit(solution)/shard_map/all_to_all | solution.py:32
  121.9 60.8 %reduce-scatter.3.cloned.1.call-start = ((), (), s32[]{:S(2)}) async-start(), calls=%async_computation.6 | async-start | bytes 589824 | tf_op jit(solution)/shard_map/reduce_scatter | solution.py:52
  131.3 22.9 %collective-permute-start.8 = (f32[64,256]{1,0:T(8,128)S(1)}, f32[64,256]{1,0:T(8,128)S(1)}, u32[]{:S(2)}, u32[]{:S(2)}) collective-permute-start(f32[64,256]{1,0:T(8,128)S(1)} %get-tuple-element.16), channel_id=1, source_target_pairs={{760,0},{0,8},{8,16},{16,24},{24,32},{32,40},{40,48},{48,56},{56,6... | collective-permute-start | bytes 196616 | tf_op jit(solution)/shard_map/ppermute | solution.py:14
  133.2 22.9 %collective-permute-start.15 = (f32[64,256]{1,0:T(8,128)S(1)}, f32[64,256]{1,0:T(8,128)S(1)}, u32[]{:S(2)}, u32[]{:S(2)}) collective-permute-start(f32[64,256]{1,0:T(8,128)S(1)} %get-tuple-element.17), channel_id=1, source_target_pairs={{704,0},{712,8},{720,16},{728,24},{736,32},{744,40},{752,48},{760,... | collective-permute-start | bytes 196616 | tf_op jit(solution)/shard_map/ppermute | solution.py:14
  135.1 23.5 %collective-permute-start.14 = (f32[64,256]{1,0:T(8,128)S(1)}, f32[64,256]{1,0:T(8,128)S(1)}, u32[]{:S(2)}, u32[]{:S(2)}) collective-permute-start(f32[64,256]{1,0:T(8,128)S(1)} %get-tuple-element.18), channel_id=1, source_target_pairs={{712,0},{720,8},{728,16},{736,24},{744,32},{752,40},{760,48},{0,56... | collective-permute-start | bytes 196616 | tf_op jit(solution)/shard_map/ppermute | solution.py:14
  138.6 22.2 %collective-permute-start.13 = (f32[64,256]{1,0:T(8,128)S(1)}, f32[64,256]{1,0:T(8,128)S(1)}, u32[]{:S(2)}, u32[]{:S(2)}) collective-permute-start(f32[64,256]{1,0:T(8,128)S(1)} %get-tuple-element.19), channel_id=1, source_target_pairs={{720,0},{728,8},{736,16},{744,24},{752,32},{760,40},{0,48},{8,56},... | collective-permute-start | bytes 196616 | tf_op jit(solution)/shard_map/ppermute | solution.py:14
  154.2 13.8 %collective-permute-start.11 = (f32[64,256]{1,0:T(8,128)S(1)}, f32[64,256]{1,0:T(8,128)S(1)}, u32[]{:S(2)}, u32[]{:S(2)}) collective-permute-start(f32[64,256]{1,0:T(8,128)S(1)} %get-tuple-element.21), channel_id=1, source_target_pairs={{736,0},{744,8},{752,16},{760,24},{0,32},{8,40},{16,48},{24,56},{3... | collective-permute-start | bytes 196616 | tf_op jit(solution)/shard_map/ppermute | solution.py:14
  158.6 13.8 %collective-permute-start.9 = (f32[64,256]{1,0:T(8,128)S(1)}, f32[64,256]{1,0:T(8,128)S(1)}, u32[]{:S(2)}, u32[]{:S(2)}) collective-permute-start(f32[64,256]{1,0:T(8,128)S(1)} %get-tuple-element.23), channel_id=1, source_target_pairs={{752,0},{760,8},{0,16},{8,24},{16,32},{24,40},{32,48},{40,56},{48,... | collective-permute-start | bytes 196616 | tf_op jit(solution)/shard_map/ppermute | solution.py:14
  183.6 15.6 %collective-permute-start.16 = (f32[64,256]{1,0:T(8,128)S(1)}, f32[64,256]{1,0:T(8,128)S(1)}, u32[]{:S(2)}, u32[]{:S(2)}) collective-permute-start(f32[64,256]{1,0:T(8,128)S(1)} %multiply_subtract_fusion.1), channel_id=1, source_target_pairs={{8,0},{16,8},{24,16},{32,24},{40,32},{48,40},{56,48},{64,56},{72,6... | collective-permute-start | bytes 196616 | tf_op jit(solution)/shard_map/ppermute | solution.py:14
  185.5 36.0 %collective-permute-start.23 = (f32[64,256]{1,0:T(8,128)S(1)}, f32[64,256]{1,0:T(8,128)S(1)}, u32[]{:S(2)}, u32[]{:S(2)}) collective-permute-start(f32[64,256]{1,0:T(8,128)S(1)} %multiply_subtract_fusion.1), channel_id=1, source_target_pairs={{64,0},{72,8},{80,16},{88,24},{96,32},{104,40},{112,48},{120,56},{... | collective-permute-start | bytes 196616 | tf_op jit(solution)/shard_map/ppermute | solution.py:14
  187.4 34.1 %collective-permute-start.22 = (f32[64,256]{1,0:T(8,128)S(1)}, f32[64,256]{1,0:T(8,128)S(1)}, u32[]{:S(2)}, u32[]{:S(2)}) collective-permute-start(f32[64,256]{1,0:T(8,128)S(1)} %multiply_subtract_fusion.1), channel_id=1, source_target_pairs={{56,0},{64,8},{72,16},{80,24},{88,32},{96,40},{104,48},{112,56},{1... | collective-permute-start | bytes 196616 | tf_op jit(solution)/shard_map/ppermute | solution.py:14
  189.4 32.1 %collective-permute-start.21 = (f32[64,256]{1,0:T(8,128)S(1)}, f32[64,256]{1,0:T(8,128)S(1)}, u32[]{:S(2)}, u32[]{:S(2)}) collective-permute-start(f32[64,256]{1,0:T(8,128)S(1)} %multiply_subtract_fusion.1), channel_id=1, source_target_pairs={{48,0},{56,8},{64,16},{72,24},{80,32},{88,40},{96,48},{104,56},{11... | collective-permute-start | bytes 196616 | tf_op jit(solution)/shard_map/ppermute | solution.py:14
  193.7 27.8 %collective-permute-start.20 = (f32[64,256]{1,0:T(8,128)S(1)}, f32[64,256]{1,0:T(8,128)S(1)}, u32[]{:S(2)}, u32[]{:S(2)}) collective-permute-start(f32[64,256]{1,0:T(8,128)S(1)} %multiply_subtract_fusion.1), channel_id=1, source_target_pairs={{40,0},{48,8},{56,16},{64,24},{72,32},{80,40},{88,48},{96,56},{104... | collective-permute-start | bytes 196616 | tf_op jit(solution)/shard_map/ppermute | solution.py:14
  223.1 41.6 %all-to-all-start.2 = ((f32[8,64,256]{2,1,0:T(8,128)}), f32[8,64,256]{2,1,0:T(8,128)S(1)}, u32[]{:S(2)}, u32[]{:S(2)}) async-start(f32[8,64,256]{2,1,0:T(8,128)} %broadcast_select_fusion.1), calls=%async_computation.3 | async-start | bytes 1048576 | tf_op jit(solution)/shard_map/all_to_all | solution.py:32
  271.1 65.1 %reduce-scatter.5.cloned.1.call-start = ((), (), s32[]{:S(2)}) async-start(), calls=%async_computation.7 | async-start | bytes 589824 | tf_op jit(solution)/shard_map/reduce_scatter | solution.py:52
  280.5 27.8 %collective-permute-start.24 = (f32[64,256]{1,0:T(8,128)S(1)}, f32[64,256]{1,0:T(8,128)S(1)}, u32[]{:S(2)}, u32[]{:S(2)}) collective-permute-start(f32[64,256]{1,0:T(8,128)S(1)} %get-tuple-element.8), channel_id=1, source_target_pairs={{760,0},{0,8},{8,16},{16,24},{24,32},{32,40},{40,48},{48,56},{56,6... | collective-permute-start | bytes 196616 | tf_op jit(solution)/shard_map/ppermute | solution.py:14
  282.4 27.8 %collective-permute-start.31 = (f32[64,256]{1,0:T(8,128)S(1)}, f32[64,256]{1,0:T(8,128)S(1)}, u32[]{:S(2)}, u32[]{:S(2)}) collective-permute-start(f32[64,256]{1,0:T(8,128)S(1)} %get-tuple-element.9), channel_id=1, source_target_pairs={{704,0},{712,8},{720,16},{728,24},{736,32},{744,40},{752,48},{760,... | collective-permute-start | bytes 196616 | tf_op jit(solution)/shard_map/ppermute | solution.py:14
  286.6 26.1 %collective-permute-start.30 = (f32[64,256]{1,0:T(8,128)S(1)}, f32[64,256]{1,0:T(8,128)S(1)}, u32[]{:S(2)}, u32[]{:S(2)}) collective-permute-start(f32[64,256]{1,0:T(8,128)S(1)} %get-tuple-element.10), channel_id=1, source_target_pairs={{712,0},{720,8},{728,16},{736,24},{744,32},{752,40},{760,48},{0,56... | collective-permute-start | bytes 196616 | tf_op jit(solution)/shard_map/ppermute | solution.py:14
  291.3 23.6 %collective-permute-start.29 = (f32[64,256]{1,0:T(8,128)S(1)}, f32[64,256]{1,0:T(8,128)S(1)}, u32[]{:S(2)}, u32[]{:S(2)}) collective-permute-start(f32[64,256]{1,0:T(8,128)S(1)} %get-tuple-element.11), channel_id=1, source_target_pairs={{720,0},{728,8},{736,16},{744,24},{752,32},{760,40},{0,48},{8,56},... | collective-permute-start | bytes 196616 | tf_op jit(solution)/shard_map/ppermute | solution.py:14
  (17 other events, 152.2 us)
Sparse Core Ops, SparseCore 0:
  125.8 56.8 reduce-scatter.2
  275.4 60.8 reduce-scatter.4
where the time goes:
time: 346 us; the launch traced here: 345 us
  starting transfers between devices  149 us (43%)
  blocking collectives  81 us (23%)
  waiting for transfers between devices  77.6 us (22%)
  between operations  14.7 us (4%)
  matrix products  11.1 us (3%)
  local copies, waits for them, and re-layouts  5.71 us (2%)
  other arithmetic  5.38 us (2%)
    ppermute x32, starting transfers between devices, passed_along(): return lax.ppermute(block, axis, route)  132 us
    all_gather x2, blocking collectives, body(): own = lax.all_gather(current, 'narrow', axis=0, tiled=True)  69.3 us
    ppermute x32, waiting for transfers between devices, passed_along(): return lax.ppermute(block, axis, route)  46.2 us
    reduce_scatter x2, waiting for transfers between devices, body(): mine = lax.psum_scatter(row_grad, 'narrow', scatter_dimension=0, tiled=True)  20.7 us
    all_gather x1, blocking collectives, body(): all_dist = lax.all_gather(tile_offset[0], 'narrow', axis=0, tiled=True) + 1  11.7 us
    all_to_all x2, waiting for transfers between devices, body(): lax.all_to_all(back.reshape(lane_count, rows_dev, width), 'narrow', split...  10.7 us
    all_to_all x2, starting transfers between devices, body(): lax.all_to_all(outgoing, 'narrow', split_axis=0, concat_axis=0, tiled=True)  9.91 us
    all_to_all x2, starting transfers between devices, body(): lax.all_to_all(back.reshape(lane_count, rows_dev, width), 'narrow', split...  6.98 us
  transfers between devices with their start and end apart: 38, of which 18 were waited for; matrix products, arithmetic and copies ran while one was open for 3% of the time, Pallas kernels for 0%

commit v1 on v0

v1 whole, which is shorter than its diff:
```python
import functools
import math

import jax
import jax.numpy as jnp
from jax import lax
from jax.experimental import pallas as pl
from jax.experimental.pallas import tpu as pltpu
from jax.sharding import PartitionSpec as P

ITERS = 2
CHUNKS = 2
MESH = pl.DeviceIdType.MESH
F32, BF16 = jnp.float32, jnp.bfloat16
NT = (((1,), (1,)), ((), ()))
TN = (((0,), (0,)), ((), ()))
NN = (((1,), (0,)), ((), ()))


def halves(a):
    hi = a.astype(BF16)
    return hi, (a - hi.astype(F32)).astype(BF16)


def dot3(a_hi, a_lo, b_hi, b_lo, dims):
    dot = functools.partial(lax.dot_general, dimension_numbers=dims, preferred_element_type=F32)
    return dot(a_hi, b_hi) + (dot(a_hi, b_lo) + dot(a_lo, b_hi))


def kernel(
    lanes, wides, rate,
    emb_ref, x_ref, c_ref, off_ref, out_ref,
    off_v, xs, cs, xr, cr, ew, near, ew_hi, ew_lo, f_hi, f_lo, w_hi, w_lo,
    back, sib_part, total, arrived, row_part, row_got,
    off_s, off_r, x_s, x_r, c_s, c_r, ag_s, ag_r, ch_s, ch_r, sb_s, sb_r,
    bs_s, bs_r, bc_s, bc_r, rs_s, rs_r,
):
    rows, width = emb_ref.shape
    block = rows * lanes
    steps = lanes // 2
    part = rows // CHUNKS
    w = lax.axis_index("wide")
    k = lax.axis_index("narrow")
    core = lax.rem(w, 2)
    below = lax.rem(w + wides - 2, wides)
    above = lax.rem(w + 2, wides)
    sibling = w + 1 - 2 * core

    def peer(r):
        return lax.rem(k + r, lanes)

    def copy(src, dst, send, recv, wide, narrow):
        return pltpu.make_async_remote_copy(
            src_ref=src, dst_ref=dst, send_sem=send, recv_sem=recv,
            device_id=(wide, narrow), device_id_type=MESH,
        )

    def over_peers(fn):
        def step(r, carry):
            fn(peer(r))
            return carry
        lax.fori_loop(1, lanes, step, 0)

    barrier = pltpu.get_barrier_semaphore()
    over_peers(lambda m: pl.semaphore_signal(barrier, inc=1, device_id=(w, m), device_id_type=MESH))
    for other in (below, above, sibling):
        pl.semaphore_signal(barrier, inc=1, device_id=(other, k), device_id_type=MESH)
    pl.semaphore_wait(barrier, lanes + 2)

    def rows_of(q):
        return pl.ds(q * part, part)

    def gather(it, m, slot):
        return copy(near.at[it, 0], ew.at[it, slot], ag_s.at[it, m], ag_r.at[it, slot], w, m)

    def chain(it, t, q):
        return copy(
            near.at[it, 2 * t, rows_of(q)], near.at[it, 2 * t + 2, rows_of(q)],
            ch_s.at[it, t, q], ch_r.at[it, t, q], below, k,
        )

    def to_sibling(it, t, q):
        return copy(
            near.at[it, 2 * t + 2 - 2 * core, rows_of(q)], near.at[it, 2 * t + 1, rows_of(q)],
            sb_s.at[it, t, q], sb_r.at[it, t, q], sibling, k,
        )

    def offsets(m, slot):
        return copy(off_v.at[k], off_v.at[slot], off_s.at[m], off_r.at[slot], w, m)

    def x_copy(m, slot):
        return copy(xs.at[m], xr.at[slot], x_s.at[m], x_r.at[slot], w, m)

    def c_copy(m, slot):
        return copy(cs.at[m], cr.at[slot], c_s.at[m], c_r.at[slot], w, m)

    def back_sibling(it, t):
        return copy(
            back.at[it, 2 * t], sib_part.at[it, t + core], bs_s.at[it, t], bs_r.at[it, t], sibling, k
        )

    def back_chain(it, v, q):
        return copy(
            total.at[it, v, rows_of(q)], arrived.at[it, v, rows_of(q)],
            bc_s.at[it, v, q], bc_r.at[it, v, q], above, k,
        )

    def scatter(it, m, slot):
        return copy(row_part.at[it, m], row_got.at[it, slot], rs_s.at[it, m], rs_r.at[it, slot], w, m)

    def start_forward(it, value):
        near[it, 0] = value
        ew[it, k] = value
        for q in range(CHUNKS):
            chain(it, 0, q).start()

        @pl.when(core == 1)
        def _():
            for q in range(CHUNKS):
                to_sibling(it, 0, q).start()

        over_peers(lambda m: gather(it, m, k).start())

    def forward(it, u):
        for q in range(CHUNKS):
            chain(it, u - 1, q).wait_recv()
            if u < steps:
                chain(it, u, q).start()
                to_sibling(it, u - 1 + core, q).start()
            else:
                @pl.when(core == 0)
                def _():
                    to_sibling(it, steps - 1, q).start()

    def wait_gather(it):
        over_peers(lambda m: gather(it, m, m).wait_recv())
        hi, lo = halves(ew[it].reshape(block, width))
        ew_hi[...] = hi
        ew_lo[...] = lo

    def tile(it, u, slot_of):
        for q in range(CHUNKS):
            to_sibling(it, u - 1, q).wait_recv()
        lo_row = (2 * u - 2) * rows
        both = pl.ds(lo_row, 2 * rows)
        f = near[it, 2 * u - 1:2 * u + 1].reshape(2 * rows, width)
        fh, fl = halves(f)
        f_hi[both] = fh
        f_lo[both] = fl
        predicted = dot3(fh, fl, ew_hi[...], ew_lo[...], NT)
        for i in range(2):
            slot = slot_of[2 * u - 2 + i]
            weighted = cr[slot] * (xr[slot] - predicted[i * rows:(i + 1) * rows])
            wh, wl = halves(weighted)
            w_hi[pl.ds(lo_row + i * rows, rows)] = wh
            w_lo[pl.ds(lo_row + i * rows, rows)] = wl
        out = dot3(w_hi[both], w_lo[both], ew_hi[...], ew_lo[...], NN)
        back[it, 2 * u - 2] = out[:rows]
        back[it, 2 * u - 1] = out[rows:]
        back_sibling(it, u - 1).start()

    def wait_sibling_part(it, u):
        if u == steps:
            @pl.when(core == 0)
            def _():
                back_sibling(it, steps - 1).wait_recv()
        elif u == 0:
            @pl.when(core == 1)
            def _():
                back_sibling(it, 0).wait_recv()
        else:
            back_sibling(it, u - 1 + core).wait_recv()

    def backward(it, v):
        u = steps - v
        wait_sibling_part(it, u)
        for q in range(CHUNKS):
            here = rows_of(q)
            if v > 0:
                back_chain(it, v - 1, q).wait_recv()
            value = back[it, 2 * u - 1, here] + sib_part[it, u, here]
            if v > 0:
                value = value + arrived[it, v - 1, here]
            total[it, v, here] = value
            back_chain(it, v, q).start()

    def row_terms(it):
        terms = dot3(w_hi[...], w_lo[...], f_hi[...], f_lo[...], TN)
        row_part[it] = terms.reshape(lanes, rows, width)
        row_got[it, k] = row_part[it, k]
        over_peers(lambda m: scatter(it, m, k).start())

    def finish(it):
        over_peers(lambda m: scatter(it, m, m).wait_recv())
        grad = row_got[it, 0]
        for m in range(1, lanes):
            grad = grad + row_got[it, m]
        wait_sibling_part(it, 0)
        grad = grad + sib_part[it, 0]
        for q in range(CHUNKS):
            back_chain(it, steps - 1, q).wait_recv()
        grad = grad + arrived[it, steps - 1]
        return near[it, 0] + rate * grad

    off_v[k] = jnp.full(off_v.shape[1:], off_ref[0, 0], jnp.int32)
    start_forward(0, emb_ref[...])
    over_peers(lambda m: offsets(m, k).start())

    def transposed(m, ref):
        pick = (
            lax.broadcasted_iota(jnp.int32, (rows, block), 1)
            == lax.broadcasted_iota(jnp.int32, (rows, block), 0) + m * rows
        )
        pick = jnp.where(pick, 1.0, 0.0).astype(BF16)
        return lax.dot_general(pick, ref[...], NT, preferred_element_type=F32)

    def send_tiles(m):
        xs[m] = transposed(m, x_ref)
        x_copy(m, k).start()
        cs[m] = transposed(m, c_ref)
        c_copy(m, k).start()

    over_peers(send_tiles)
    xr[k] = transposed(k, x_ref)
    cr[k] = transposed(k, c_ref)
    for it in range(ITERS):
        sib_part[it, steps * core] = jnp.zeros((rows, width), F32)

    for it in range(ITERS):
        if it == 0:
            for u in range(1, steps + 1):
                forward(it, u)
            wait_gather(it)
            over_peers(lambda m: offsets(m, m).wait_recv())
            offs = [jnp.max(off_v[s]) for s in range(lanes)]
            slot_of = []
            for d in range(lanes):
                found = jnp.int32(0)
                for s in range(1, lanes):
                    found = jnp.where(offs[s] == d, s, found)
                slot_of.append(found)
            over_peers(lambda m: x_copy(m, m).wait_recv())
            over_peers(lambda m: c_copy(m, m).wait_recv())
            tile(it, steps, slot_of)
            backward(it, 0)
            for u in range(steps - 1, 0, -1):
                tile(it, u, slot_of)
        else:
            for u in range(1, steps // 2 + 1):
                forward(it, u)
            wait_gather(it)
            for u in range(1, steps // 2 + 1):
                tile(it, u, slot_of)
            for u in range(steps // 2 + 1, steps + 1):
                forward(it, u)
                tile(it, u, slot_of)
            backward(it, 0)
        row_terms(it)
        for v in range(1, steps):
            backward(it, v)
        value = finish(it)
        if it < ITERS - 1:
            start_forward(it + 1, value)
        else:
            out_ref[...] = value

    def drain(m):
        offsets(m, k).wait_send()
        x_copy(m, k).wait_send()
        c_copy(m, k).wait_send()
        for it in range(ITERS):
            gather(it, m, k).wait_send()
            scatter(it, m, k).wait_send()

    over_peers(drain)
    for it in range(ITERS):
        for t in range(steps):
            back_sibling(it, t).wait_send()
            for q in range(CHUNKS):
                chain(it, t, q).wait_send()
                to_sibling(it, t, q).wait_send()
                back_chain(it, t, q).wait_send()


def body(embeddings, co_engagement, confidence, tile_offset):
    rows, width = embeddings.shape
    lanes = lax.axis_size("narrow")
    wides = lax.axis_size("wide")
    block = rows * lanes
    steps = lanes // 2
    rate = 0.75 * math.sqrt(width) / (lanes * block)
    vmem = pl.BlockSpec(memory_space=pltpu.VMEM)
    dma = pltpu.SemaphoreType.DMA
    return pl.pallas_call(
        functools.partial(kernel, lanes, wides, rate),
        out_shape=jax.ShapeDtypeStruct((rows, width), F32),
        in_specs=[vmem, vmem, vmem, pl.BlockSpec(memory_space=pltpu.SMEM)],
        out_specs=vmem,
        scratch_shapes=[
            pltpu.VMEM((lanes, 8, 128), jnp.int32),
            *[pltpu.VMEM((lanes, rows, block), F32)] * 4,
            pltpu.VMEM((ITERS, lanes, rows, width), F32),
            pltpu.VMEM((ITERS, lanes + 1, rows, width), F32),
            *[pltpu.VMEM((block, width), BF16)] * 4,
            *[pltpu.VMEM((block, block), BF16)] * 2,
            pltpu.VMEM((ITERS, lanes, rows, width), F32),
            pltpu.VMEM((ITERS, steps + 1, rows, width), F32),
            pltpu.VMEM((ITERS, steps, rows, width), F32),
            pltpu.VMEM((ITERS, steps, rows, width), F32),
            pltpu.VMEM((ITERS, lanes, rows, width), F32),
            pltpu.VMEM((ITERS, lanes, rows, width), F32),
            *[dma((lanes,))] * 6,
            *[dma((ITERS, lanes))] * 2,
            *[dma((ITERS, steps, CHUNKS))] * 4,
            *[dma((ITERS, steps))] * 2,
            *[dma((ITERS, steps, CHUNKS))] * 2,
            *[dma((ITERS, lanes))] * 2,
        ],
        compiler_params=pltpu.CompilerParams(
            collective_id=0, has_side_effects=True, vmem_limit_bytes=40 * 1024 * 1024
        ),
        cost_estimate=pl.CostEstimate(
            flops=ITERS * 18 * block * block * width, bytes_accessed=4 * block * block, transcendentals=0
        ),
    )(embeddings, co_engagement, confidence, tile_offset)


def solution(mesh):
    in_specs = (
        P(("wide", "narrow"), None),
        P("wide", "narrow"),
        P("wide", "narrow"),
        P("wide", "narrow"),
    )
    out_specs = P(("wide", "narrow"), None)
    return jax.shard_map(body, mesh=mesh, in_specs=in_specs, out_specs=out_specs, check_vma=False)
```

time: 346 us -> 114 us (0.33)
  the two profiles are of different devices: /device:TPU:16 before, /device:TPU:10 now
where the time goes in v1:
time: 114 us
  Pallas kernels  110 us (96%)
  local copies, waits for them, and re-layouts  3.55 us (3%)
    pallas_call x1, Pallas kernels, body(): pl.pallas_call(functools.partial(kernel, lanes, wides, rate), out_shape=j...  110 us
    unnamed x7, local copies, waits for them, and re-layouts  3.55 us

profile of v1, /device:TPU:10, one launch (start us, length us, event | category | flops | bytes accessed | tf_op | source)
XLA Modules:
  0.0 114.0 jit_solution(3405192447394183932)
XLA Ops:
  0.7 0.0 copy-start
  0.7 1.0 copy-done
  1.7 0.0 copy-start.1
  1.7 1.0 copy-done.1
  2.7 0.0 copy-start.2
  2.7 0.8 copy-done.2
  3.6 109.8 %shard_map.46 = f32[64,256]{1,0:T(8,128)S(1)} custom-call(f32[64,256]{1,0:T(8,128)S(1)} %copy-done.2, bf16[512,512]{1,0:T(8,128)(2,1)S(1)} %copy-done, bf16[512,512]{1,0:T(8,128)(2,1)S(1)} %copy-done.1, s32[1,1]{1,0:T(1,128)S(6)} %copy.6.off_ref), custom_call_target="tpu_custom_call" | custom-call | flops 2415919104 | bytes 1048576 | tf_op jit(solution)/shard_map/pallas_call | solution.py:294
  113.4 0.6 copy.7
Async XLA Ops:
  0.7 1.0 copy-start
  1.7 1.0 copy-start.1
  2.7 0.8 copy-start.2

commit v2 on v1

--- a/solution.py
+++ b/solution.py
@@ -31,8 +31,8 @@
     lanes, wides, rate,
     emb_ref, x_ref, c_ref, off_ref, out_ref,
     off_v, xs, cs, xr, cr, ew, near, ew_hi, ew_lo, f_hi, f_lo, w_hi, w_lo,
-    back, sib_part, total, arrived, row_part, row_got,
-    off_s, off_r, x_s, x_r, c_s, c_r, ag_s, ag_r, ch_s, ch_r, sb_s, sb_r,
+    back, sib_part, total, arrived, row_part, row_got, x_in, c_in, pred,
+    in_s, off_s, off_r, x_s, x_r, c_s, c_r, ag_s, ag_r, ch_s, ch_r, sb_s, sb_r,
     bs_s, bs_r, bc_s, bc_r, rs_s, rs_r,
 ):
     rows, width = emb_ref.shape
@@ -61,17 +61,35 @@
             return carry
         lax.fori_loop(1, lanes, step, 0)
 
+    e_load = pltpu.make_async_copy(emb_ref, near.at[0, 0], in_s.at[0])
+    x_load = pltpu.make_async_copy(x_ref, x_in, in_s.at[1])
+    c_load = pltpu.make_async_copy(c_ref, c_in, in_s.at[2])
     barrier = pltpu.get_barrier_semaphore()
     over_peers(lambda m: pl.semaphore_signal(barrier, inc=1, device_id=(w, m), device_id_type=MESH))
     for other in (below, above, sibling):
         pl.semaphore_signal(barrier, inc=1, device_id=(other, k), device_id_type=MESH)
+    e_load.start()
+    x_load.start()
+    c_load.start()
+    off_v[k] = jnp.full(off_v.shape[1:], off_ref[0, 0], jnp.int32)
+    for it in range(ITERS):
+        sib_part[it, steps * core] = jnp.zeros((rows, width), F32)
+    e_load.wait()
     pl.semaphore_wait(barrier, lanes + 2)
 
     def rows_of(q):
         return pl.ds(q * part, part)
 
-    def gather(it, m, slot):
-        return copy(near.at[it, 0], ew.at[it, slot], ag_s.at[it, m], ag_r.at[it, slot], w, m)
+    def gather(it, i, m, piece):
+        src = near.at[it, 0] if i < lanes // 2 else ew.at[it, piece]
+        return copy(src, ew.at[it, piece], ag_s.at[it, i], ag_r.at[it, piece], w, m)
+
+    neighbour = k + 1 - 2 * lax.rem(k, 2)
+
+    def pass_on(it):
+        gather(it, 0, neighbour, neighbour).wait_recv()
+        for i in range(1, lanes // 2):
+            gather(it, lanes // 2 - 1 + i, peer(2 * i), neighbour).start()
 
     def chain(it, t, q):
         return copy(
@@ -108,9 +126,7 @@
     def scatter(it, m, slot):
         return copy(row_part.at[it, m], row_got.at[it, slot], rs_s.at[it, m], rs_r.at[it, slot], w, m)
 
-    def start_forward(it, value):
-        near[it, 0] = value
-        ew[it, k] = value
+    def start_forward(it):
         for q in range(CHUNKS):
             chain(it, 0, q).start()
 
@@ -119,7 +135,9 @@
             for q in range(CHUNKS):
                 to_sibling(it, 0, q).start()
 
-        over_peers(lambda m: gather(it, m, k).start())
+        for i in range(lanes // 2):
+            gather(it, i, peer(2 * i) if i else neighbour, k).start()
+        ew[it, k] = near[it, 0]
 
     def forward(it, u):
         for q in range(CHUNKS):
@@ -133,31 +151,34 @@
                     to_sibling(it, steps - 1, q).start()
 
     def wait_gather(it):
-        over_peers(lambda m: gather(it, m, m).wait_recv())
+        over_peers(
+            lambda m: pl.when(m != neighbour)(lambda: gather(it, 1, m, m).wait_recv())
+        )
         hi, lo = halves(ew[it].reshape(block, width))
         ew_hi[...] = hi
         ew_lo[...] = lo
 
-    def tile(it, u, slot_of):
-        for q in range(CHUNKS):
-            to_sibling(it, u - 1, q).wait_recv()
-        lo_row = (2 * u - 2) * rows
-        both = pl.ds(lo_row, 2 * rows)
-        f = near[it, 2 * u - 1:2 * u + 1].reshape(2 * rows, width)
-        fh, fl = halves(f)
-        f_hi[both] = fh
-        f_lo[both] = fl
-        predicted = dot3(fh, fl, ew_hi[...], ew_lo[...], NT)
-        for i in range(2):
-            slot = slot_of[2 * u - 2 + i]
-            weighted = cr[slot] * (xr[slot] - predicted[i * rows:(i + 1) * rows])
-            wh, wl = halves(weighted)
-            w_hi[pl.ds(lo_row + i * rows, rows)] = wh
-            w_lo[pl.ds(lo_row + i * rows, rows)] = wl
-        out = dot3(w_hi[both], w_lo[both], ew_hi[...], ew_lo[...], NN)
-        back[it, 2 * u - 2] = out[:rows]
-        back[it, 2 * u - 1] = out[rows:]
-        back_sibling(it, u - 1).start()
+    def predict(it, first, last):
+        for t in range(first - 1, last):
+            for q in range(CHUNKS):
+                to_sibling(it, t, q).wait_recv()
+        some = pl.ds((2 * first - 2) * rows, 2 * (last - first + 1) * rows)
+        fh, fl = halves(near[it, 2 * first - 1:2 * last + 1].reshape(some.size, width))
+        f_hi[some] = fh
+        f_lo[some] = fl
+        pred[some] = dot3(fh, fl, ew_hi[...], ew_lo[...], NT)
+
+    def tile(it, first, last, slot_of):
+        some = pl.ds((2 * first - 2) * rows, 2 * (last - first + 1) * rows)
+        for d in range(2 * first - 2, 2 * last):
+            here = pl.ds(d * rows, rows)
+            wh, wl = halves(cr[slot_of[d]] * (xr[slot_of[d]] - pred[here]))
+            w_hi[here] = wh
+            w_lo[here] = wl
+        out = dot3(w_hi[some], w_lo[some], ew_hi[...], ew_lo[...], NN)
+        back[it, 2 * first - 2:2 * last] = out.reshape(2 * (last - first + 1), rows, width)
+        for u in range(first, last + 1):
+            back_sibling(it, u - 1).start()
 
     def wait_sibling_part(it, u):
         if u == steps:
@@ -190,47 +211,50 @@
         row_got[it, k] = row_part[it, k]
         over_peers(lambda m: scatter(it, m, k).start())
 
-    def finish(it):
+    def finish(it, store):
         over_peers(lambda m: scatter(it, m, m).wait_recv())
-        grad = row_got[it, 0]
+        wait_sibling_part(it, 0)
+        grad = row_got[it, 0] + sib_part[it, 0]
         for m in range(1, lanes):
             grad = grad + row_got[it, m]
-        wait_sibling_part(it, 0)
-        grad = grad + sib_part[it, 0]
         for q in range(CHUNKS):
+            here = rows_of(q)
             back_chain(it, steps - 1, q).wait_recv()
-        grad = grad + arrived[it, steps - 1]
-        return near[it, 0] + rate * grad
-
-    off_v[k] = jnp.full(off_v.shape[1:], off_ref[0, 0], jnp.int32)
-    start_forward(0, emb_ref[...])
+            store(here, near[it, 0, here] + rate * (grad[q * part:(q + 1) * part] + arrived[it, steps - 1, here]))
+
+    def keep(here, value):
+        near[1, 0, here] = value
+
+    def result(here, value):
+        out_ref[here] = value
+
+    start_forward(0)
     over_peers(lambda m: offsets(m, k).start())
 
-    def transposed(m, ref):
-        pick = (
-            lax.broadcasted_iota(jnp.int32, (rows, block), 1)
-            == lax.broadcasted_iota(jnp.int32, (rows, block), 0) + m * rows
-        )
-        pick = jnp.where(pick, 1.0, 0.0).astype(BF16)
-        return lax.dot_general(pick, ref[...], NT, preferred_element_type=F32)
-
-    def send_tiles(m):
-        xs[m] = transposed(m, x_ref)
-        x_copy(m, k).start()
-        cs[m] = transposed(m, c_ref)
-        c_copy(m, k).start()
-
-    over_peers(send_tiles)
-    xr[k] = transposed(k, x_ref)
-    cr[k] = transposed(k, c_ref)
-    for it in range(ITERS):
-        sib_part[it, steps * core] = jnp.zeros((rows, width), F32)
+    def transpose(ref, out):
+        eye = (
+            lax.broadcasted_iota(jnp.int32, (block, block), 0)
+            == lax.broadcasted_iota(jnp.int32, (block, block), 1)
+        )
+        eye = jnp.where(eye, 1.0, 0.0).astype(BF16)
+        out[...] = lax.dot_general(eye, ref[...], NT, preferred_element_type=F32).reshape(out.shape)
+
+    x_load.wait()
+    transpose(x_in, xs)
+    over_peers(lambda m: x_copy(m, k).start())
+    c_load.wait()
+    transpose(c_in, cs)
+    pass_on(0)
+    over_peers(lambda m: c_copy(m, k).start())
+    xr[k] = xs[k]
+    cr[k] = cs[k]
 
     for it in range(ITERS):
         if it == 0:
             for u in range(1, steps + 1):
                 forward(it, u)
             wait_gather(it)
+            predict(it, 1, steps)
             over_peers(lambda m: offsets(m, m).wait_recv())
             offs = [jnp.max(off_v[s]) for s in range(lanes)]
             slot_of = []
@@ -241,39 +265,38 @@
                 slot_of.append(found)
             over_peers(lambda m: x_copy(m, m).wait_recv())
             over_peers(lambda m: c_copy(m, m).wait_recv())
-            tile(it, steps, slot_of)
-            backward(it, 0)
-            for u in range(steps - 1, 0, -1):
-                tile(it, u, slot_of)
+            tile(it, steps, steps, slot_of)
+            tile(it, 1, steps - 1, slot_of)
         else:
-            for u in range(1, steps // 2 + 1):
+            pass_on(it)
+            for u in range(1, steps + 1):
                 forward(it, u)
-            wait_gather(it)
-            for u in range(1, steps // 2 + 1):
-                tile(it, u, slot_of)
-            for u in range(steps // 2 + 1, steps + 1):
-                forward(it, u)
-                tile(it, u, slot_of)
-            backward(it, 0)
+                if u == 2:
+                    wait_gather(it)
+                    predict(it, 1, 1)
+                    tile(it, 1, 1, slot_of)
+                if u >= 2:
+                    predict(it, u, u)
+                    tile(it, u, u, slot_of)
+        backward(it, 0)
         row_terms(it)
         for v in range(1, steps):
             backward(it, v)
-        value = finish(it)
+        finish(it, keep if it < ITERS - 1 else result)
         if it < ITERS - 1:
-            start_forward(it + 1, value)
-        else:
-            out_ref[...] = value
+            start_forward(it + 1)
 
     def drain(m):
         offsets(m, k).wait_send()
         x_copy(m, k).wait_send()
         c_copy(m, k).wait_send()
         for it in range(ITERS):
-            gather(it, m, k).wait_send()
             scatter(it, m, k).wait_send()
 
     over_peers(drain)
     for it in range(ITERS):
+        for i in range(lanes - 1):
+            gather(it, i, neighbour, k if i < lanes // 2 else neighbour).wait_send()
         for t in range(steps):
             back_sibling(it, t).wait_send()
             for q in range(CHUNKS):
@@ -290,11 +313,12 @@
     steps = lanes // 2
     rate = 0.75 * math.sqrt(width) / (lanes * block)
     vmem = pl.BlockSpec(memory_space=pltpu.VMEM)
+    hbm = pl.BlockSpec(memory_space=pltpu.HBM)
     dma = pltpu.SemaphoreType.DMA
     return pl.pallas_call(
         functools.partial(kernel, lanes, wides, rate),
         out_shape=jax.ShapeDtypeStruct((rows, width), F32),
-        in_specs=[vmem, vmem, vmem, pl.BlockSpec(memory_space=pltpu.SMEM)],
+        in_specs=[hbm, hbm, hbm, pl.BlockSpec(memory_space=pltpu.SMEM)],
         out_specs=vmem,
         scratch_shapes=[
             pltpu.VMEM((lanes, 8, 128), jnp.int32),
@@ -309,6 +333,9 @@
             pltpu.VMEM((ITERS, steps, rows, width), F32),
             pltpu.VMEM((ITERS, lanes, rows, width), F32),
             pltpu.VMEM((ITERS, lanes, rows, width), F32),
+            *[pltpu.VMEM((block, block), BF16)] * 2,
+            pltpu.VMEM((block, block), F32),
+            dma((3,)),
             *[dma((lanes,))] * 6,
             *[dma((ITERS, lanes))] * 2,
             *[dma((ITERS, steps, CHUNKS))] * 4,
@@ -317,7 +344,7 @@
             *[dma((ITERS, lanes))] * 2,
         ],
         compiler_params=pltpu.CompilerParams(
-            collective_id=0, has_side_effects=True, vmem_limit_bytes=40 * 1024 * 1024
+            collective_id=0, has_side_effects=True, vmem_limit_bytes=63 * 1024 * 1024
         ),
         cost_estimate=pl.CostEstimate(
             flops=ITERS * 18 * block * block * width, bytes_accessed=4 * block * block, transcendentals=0

time: 114 us -> 110 us (0.965)
  the two profiles are of different devices: /device:TPU:10 before, /device:TPU:9 now
where the time goes in v2:
time: 110 us
  Pallas kernels  108 us (98%)
  local copies, waits for them, and re-layouts  1.47 us (1%)
    pallas_call x1, Pallas kernels, body(): pl.pallas_call(functools.partial(kernel, lanes, wides, rate), out_shape=j...  108 us

profile of v2, /device:TPU:9, one launch (start us, length us, event | category | flops | bytes accessed | tf_op | source)
XLA Modules:
  0.0 109.7 jit_solution(7217432935916436877)
XLA Ops:
  0.7 107.5 %shard_map.46 = f32[64,256]{1,0:T(8,128)} custom-call(f32[64,256]{1,0:T(8,128)} %emb_ref.1, bf16[512,512]{1,0:T(8,128)(2,1)} %x_ref.1, bf16[512,512]{1,0:T(8,128)(2,1)} %c_ref.1, s32[1,1]{1,0:T(1,128)S(6)} %copy.6.off_ref), custom_call_target="tpu_custom_call" | custom-call | flops 2415919104 | bytes 1048576 | tf_op jit(solution)/shard_map/pallas_call | solution.py:318
  108.2 1.5 %copy.7 = f32[64,256]{1,0:T(8,128)} copy(f32[64,256]{1,0:T(8,128)} %shard_map.46) | data formatting | bytes 131072

commit v3 on v2

--- a/solution.py
+++ b/solution.py
@@ -9,7 +9,8 @@
 from jax.sharding import PartitionSpec as P
 
 ITERS = 2
-CHUNKS = 2
+CHUNKS = 1
+HOP = {1: 1, 2: 2, 3: 1, 4: 2}
 MESH = pl.DeviceIdType.MESH
 F32, BF16 = jnp.float32, jnp.bfloat16
 NT = (((1,), (1,)), ((), ()))
@@ -42,8 +43,8 @@
     w = lax.axis_index("wide")
     k = lax.axis_index("narrow")
     core = lax.rem(w, 2)
-    below = lax.rem(w + wides - 2, wides)
-    above = lax.rem(w + 2, wides)
+    below = {g: lax.rem(w + wides - 2 * g, wides) for g in (1, 2)}
+    above = {g: lax.rem(w + 2 * g, wides) for g in (1, 2)}
     sibling = w + 1 - 2 * core
 
     def peer(r):
@@ -66,7 +67,7 @@
     c_load = pltpu.make_async_copy(c_ref, c_in, in_s.at[2])
     barrier = pltpu.get_barrier_semaphore()
     over_peers(lambda m: pl.semaphore_signal(barrier, inc=1, device_id=(w, m), device_id_type=MESH))
-    for other in (below, above, sibling):
+    for other in (*below.values(), *above.values(), sibling):
         pl.semaphore_signal(barrier, inc=1, device_id=(other, k), device_id_type=MESH)
     e_load.start()
     x_load.start()
@@ -75,7 +76,7 @@
     for it in range(ITERS):
         sib_part[it, steps * core] = jnp.zeros((rows, width), F32)
     e_load.wait()
-    pl.semaphore_wait(barrier, lanes + 2)
+    pl.semaphore_wait(barrier, lanes + 4)
 
     def rows_of(q):
         return pl.ds(q * part, part)
@@ -91,10 +92,10 @@
         for i in range(1, lanes // 2):
             gather(it, lanes // 2 - 1 + i, peer(2 * i), neighbour).start()
 
-    def chain(it, t, q):
+    def down(it, h, q):
         return copy(
-            near.at[it, 2 * t, rows_of(q)], near.at[it, 2 * t + 2, rows_of(q)],
-            ch_s.at[it, t, q], ch_r.at[it, t, q], below, k,
+            near.at[it, 2 * (h - HOP[h]), rows_of(q)], near.at[it, 2 * h, rows_of(q)],
+            ch_s.at[it, h - 1, q], ch_r.at[it, h - 1, q], below[HOP[h]], k,
         )
 
     def to_sibling(it, t, q):
@@ -117,18 +118,19 @@
             back.at[it, 2 * t], sib_part.at[it, t + core], bs_s.at[it, t], bs_r.at[it, t], sibling, k
         )
 
-    def back_chain(it, v, q):
+    def up(it, h, q):
         return copy(
-            total.at[it, v, rows_of(q)], arrived.at[it, v, rows_of(q)],
-            bc_s.at[it, v, q], bc_r.at[it, v, q], above, k,
+            total.at[it, h - 1, rows_of(q)], arrived.at[it, h - 1, rows_of(q)],
+            bc_s.at[it, h - 1, q], bc_r.at[it, h - 1, q], above[HOP[h]], k,
         )
 
     def scatter(it, m, slot):
         return copy(row_part.at[it, m], row_got.at[it, slot], rs_s.at[it, m], rs_r.at[it, slot], w, m)
 
     def start_forward(it):
-        for q in range(CHUNKS):
-            chain(it, 0, q).start()
+        for h in (2, 1):
+            for q in range(CHUNKS):
+                down(it, h, q).start()
 
         @pl.when(core == 1)
         def _():
@@ -141,9 +143,11 @@
 
     def forward(it, u):
         for q in range(CHUNKS):
-            chain(it, u - 1, q).wait_recv()
+            down(it, u, q).wait_recv()
+            if u == 2:
+                down(it, 4, q).start()
+                down(it, 3, q).start()
             if u < steps:
-                chain(it, u, q).start()
                 to_sibling(it, u - 1 + core, q).start()
             else:
                 @pl.when(core == 0)
@@ -192,18 +196,17 @@
         else:
             back_sibling(it, u - 1 + core).wait_recv()
 
-    def backward(it, v):
-        u = steps - v
-        wait_sibling_part(it, u)
+    def backward(it, h):
+        wait_sibling_part(it, h)
         for q in range(CHUNKS):
             here = rows_of(q)
-            if v > 0:
-                back_chain(it, v - 1, q).wait_recv()
-            value = back[it, 2 * u - 1, here] + sib_part[it, u, here]
-            if v > 0:
-                value = value + arrived[it, v - 1, here]
-            total[it, v, here] = value
-            back_chain(it, v, q).start()
+            value = back[it, 2 * h - 1, here] + sib_part[it, h, here]
+            if h == 2:
+                for far in (3, 4):
+                    up(it, far, q).wait_recv()
+                    value = value + arrived[it, far - 1, here]
+            total[it, h - 1, here] = value
+            up(it, h, q).start()
 
     def row_terms(it):
         terms = dot3(w_hi[...], w_lo[...], f_hi[...], f_lo[...], TN)
@@ -219,8 +222,11 @@
             grad = grad + row_got[it, m]
         for q in range(CHUNKS):
             here = rows_of(q)
-            back_chain(it, steps - 1, q).wait_recv()
-            store(here, near[it, 0, here] + rate * (grad[q * part:(q + 1) * part] + arrived[it, steps - 1, here]))
+            terms = grad[q * part:(q + 1) * part]
+            for h in (1, 2):
+                up(it, h, q).wait_recv()
+                terms = terms + arrived[it, h - 1, here]
+            store(here, near[it, 0, here] + rate * terms)
 
     def keep(here, value):
         near[1, 0, here] = value
@@ -251,7 +257,7 @@
 
     for it in range(ITERS):
         if it == 0:
-            for u in range(1, steps + 1):
+            for u in (2, 1, 3, 4):
                 forward(it, u)
             wait_gather(it)
             predict(it, 1, steps)
@@ -269,19 +275,20 @@
             tile(it, 1, steps - 1, slot_of)
         else:
             pass_on(it)
-            for u in range(1, steps + 1):
-                forward(it, u)
-                if u == 2:
-                    wait_gather(it)
-                    predict(it, 1, 1)
-                    tile(it, 1, 1, slot_of)
-                if u >= 2:
-                    predict(it, u, u)
-                    tile(it, u, u, slot_of)
-        backward(it, 0)
+            forward(it, 2)
+            forward(it, 1)
+            wait_gather(it)
+            predict(it, 1, 2)
+            tile(it, 1, 2, slot_of)
+            forward(it, 3)
+            forward(it, 4)
+            predict(it, 3, 4)
+            tile(it, 3, 4, slot_of)
+        backward(it, 4)
+        backward(it, 3)
+        backward(it, 1)
         row_terms(it)
-        for v in range(1, steps):
-            backward(it, v)
+        backward(it, 2)
         finish(it, keep if it < ITERS - 1 else result)
         if it < ITERS - 1:
             start_forward(it + 1)
@@ -300,9 +307,9 @@
         for t in range(steps):
             back_sibling(it, t).wait_send()
             for q in range(CHUNKS):
-                chain(it, t, q).wait_send()
+                down(it, t + 1, q).wait_send()
                 to_sibling(it, t, q).wait_send()
-                back_chain(it, t, q).wait_send()
+                up(it, t + 1, q).wait_send()
 
 
 def body(embeddings, co_engagement, confidence, tile_offset):

time: 110 us -> 105 us (0.955)
  the two profiles are of different devices: /device:TPU:9 before, /device:TPU:14 now
where the time goes in v3:
time: 105 us
  Pallas kernels  103 us (98%)
  local copies, waits for them, and re-layouts  1.47 us (1%)
    pallas_call x1, Pallas kernels, body(): pl.pallas_call(functools.partial(kernel, lanes, wides, rate), out_shape=j...  103 us

profile of v3, /device:TPU:14, one launch (start us, length us, event | category | flops | bytes accessed | tf_op | source)
XLA Modules:
  0.0 104.9 jit_solution(14562236666084044255)
XLA Ops:
  0.7 102.8 %shard_map.46 = f32[64,256]{1,0:T(8,128)} custom-call(f32[64,256]{1,0:T(8,128)} %emb_ref.1, bf16[512,512]{1,0:T(8,128)(2,1)} %x_ref.1, bf16[512,512]{1,0:T(8,128)(2,1)} %c_ref.1, s32[1,1]{1,0:T(1,128)S(6)} %copy.6.off_ref), custom_call_target="tpu_custom_call" | custom-call | flops 2415919104 | bytes 1048576 | tf_op jit(solution)/shard_map/pallas_call | solution.py:325
  103.4 1.5 %copy.7 = f32[64,256]{1,0:T(8,128)} copy(f32[64,256]{1,0:T(8,128)} %shard_map.46) | data formatting | bytes 131072

commit v4 on v3

--- a/solution.py
+++ b/solution.py
@@ -284,10 +284,10 @@
             forward(it, 4)
             predict(it, 3, 4)
             tile(it, 3, 4, slot_of)
+        row_terms(it)
         backward(it, 4)
         backward(it, 3)
         backward(it, 1)
-        row_terms(it)
         backward(it, 2)
         finish(it, keep if it < ITERS - 1 else result)
         if it < ITERS - 1:
@@ -351,7 +351,7 @@
             *[dma((ITERS, lanes))] * 2,
         ],
         compiler_params=pltpu.CompilerParams(
-            collective_id=0, has_side_effects=True, vmem_limit_bytes=63 * 1024 * 1024
+            collective_id=0, has_side_effects=True, vmem_limit_bytes=54784 * 1024
         ),
         cost_estimate=pl.CostEstimate(
             flops=ITERS * 18 * block * block * width, bytes_accessed=4 * block * block, transcendentals=0

time: 105 us -> 104 us (level)
  the two profiles are of different devices: /device:TPU:14 before, /device:TPU:9 now
where the time goes in v4:
time: 104 us
  Pallas kernels  101 us (97%)
  local copies, waits for them, and re-layouts  1.46 us (1%)
    pallas_call x1, Pallas kernels, body(): pl.pallas_call(functools.partial(kernel, lanes, wides, rate), out_shape=j...  101 us

profile of v4, /device:TPU:9, one launch (start us, length us, event | category | flops | bytes accessed | tf_op | source)
XLA Modules:
  0.0 103.6 jit_solution(15773913416232249846)
XLA Ops:
  0.7 0.0 copy-start
  0.7 0.8 copy-done
  1.5 101.5 %shard_map.46 = f32[64,256]{1,0:T(8,128)S(1)} custom-call(f32[64,256]{1,0:T(8,128)S(1)} %copy-done, bf16[512,512]{1,0:T(8,128)(2,1)} %x_ref.1, bf16[512,512]{1,0:T(8,128)(2,1)} %c_ref.1, s32[1,1]{1,0:T(1,128)S(6)} %copy.6.off_ref), custom_call_target="tpu_custom_call" | custom-call | flops 2415919104 | bytes 1048576 | tf_op jit(solution)/shard_map/pallas_call | solution.py:325
  103.0 0.6 copy.7
Async XLA Ops:
  0.7 0.8 copy-start

commit v5 on v4

--- a/solution.py
+++ b/solution.py
@@ -85,6 +85,9 @@
         src = near.at[it, 0] if i < lanes // 2 else ew.at[it, piece]
         return copy(src, ew.at[it, piece], ag_s.at[it, i], ag_r.at[it, piece], w, m)
 
+    def direct(it, m, piece):
+        return copy(near.at[it, 0], ew.at[it, piece], ag_s.at[it, m], ag_r.at[it, piece], w, m)
+
     neighbour = k + 1 - 2 * lax.rem(k, 2)
 
     def pass_on(it):
@@ -137,8 +140,11 @@
             for q in range(CHUNKS):
                 to_sibling(it, 0, q).start()
 
-        for i in range(lanes // 2):
-            gather(it, i, peer(2 * i) if i else neighbour, k).start()
+        if it == 0:
+            for i in range(lanes // 2):
+                gather(it, i, peer(2 * i) if i else neighbour, k).start()
+        else:
+            over_peers(lambda m: direct(it, m, k).start())
         ew[it, k] = near[it, 0]
 
     def forward(it, u):
@@ -155,9 +161,12 @@
                     to_sibling(it, steps - 1, q).start()
 
     def wait_gather(it):
-        over_peers(
-            lambda m: pl.when(m != neighbour)(lambda: gather(it, 1, m, m).wait_recv())
-        )
+        if it == 0:
+            over_peers(
+                lambda m: pl.when(m != neighbour)(lambda: gather(it, 1, m, m).wait_recv())
+            )
+        else:
+            over_peers(lambda m: direct(it, m, m).wait_recv())
         hi, lo = halves(ew[it].reshape(block, width))
         ew_hi[...] = hi
         ew_lo[...] = lo
@@ -181,7 +190,7 @@
             w_lo[here] = wl
         out = dot3(w_hi[some], w_lo[some], ew_hi[...], ew_lo[...], NN)
         back[it, 2 * first - 2:2 * last] = out.reshape(2 * (last - first + 1), rows, width)
-        for u in range(first, last + 1):
+        for u in range(last, first - 1, -1):
             back_sibling(it, u - 1).start()
 
     def wait_sibling_part(it, u):
@@ -274,7 +283,6 @@
             tile(it, steps, steps, slot_of)
             tile(it, 1, steps - 1, slot_of)
         else:
-            pass_on(it)
             forward(it, 2)
             forward(it, 1)
             wait_gather(it)
@@ -302,8 +310,11 @@
 
     over_peers(drain)
     for it in range(ITERS):
-        for i in range(lanes - 1):
-            gather(it, i, neighbour, k if i < lanes // 2 else neighbour).wait_send()
+        if it == 0:
+            for i in range(lanes - 1):
+                gather(it, i, neighbour, k if i < lanes // 2 else neighbour).wait_send()
+        else:
+            over_peers(lambda m: direct(it, m, k).wait_send())
         for t in range(steps):
             back_sibling(it, t).wait_send()
             for q in range(CHUNKS):

time: 104 us -> 103 us (level)
  no operation moved by 1% of the time
where the time goes in v5:
time: 103 us
  Pallas kernels  101 us (98%)
  local copies, waits for them, and re-layouts  1.46 us (1%)
    pallas_call x1, Pallas kernels, body(): pl.pallas_call(functools.partial(kernel, lanes, wides, rate), out_shape=j...  101 us

profile of v5, /device:TPU:9, one launch (start us, length us, event | category | flops | bytes accessed | tf_op | source)
XLA Modules:
  0.0 103.1 jit_solution(13527052268466211157)
XLA Ops:
  0.7 0.0 copy-start
  0.7 0.8 copy-done
  1.5 100.9 %shard_map.46 = f32[64,256]{1,0:T(8,128)S(1)} custom-call(f32[64,256]{1,0:T(8,128)S(1)} %copy-done, bf16[512,512]{1,0:T(8,128)(2,1)} %x_ref.1, bf16[512,512]{1,0:T(8,128)(2,1)} %c_ref.1, s32[1,1]{1,0:T(1,128)S(6)} %copy.6.off_ref), custom_call_target="tpu_custom_call" | custom-call | flops 2415919104 | bytes 1048576 | tf_op jit(solution)/shard_map/pallas_call | solution.py:336
  102.4 0.6 copy.7
Async XLA Ops:
  0.7 0.8 copy-start

commit v6 on v5

--- a/solution.py
+++ b/solution.py
@@ -280,8 +280,7 @@
                 slot_of.append(found)
             over_peers(lambda m: x_copy(m, m).wait_recv())
             over_peers(lambda m: c_copy(m, m).wait_recv())
-            tile(it, steps, steps, slot_of)
-            tile(it, 1, steps - 1, slot_of)
+            tile(it, 1, steps, slot_of)
         else:
             forward(it, 2)
             forward(it, 1)

time: 103 us -> 103 us (level)
  no operation moved by 1% of the time
where the time goes in v6:
time: 103 us
  Pallas kernels  101 us (98%)
  local copies, waits for them, and re-layouts  1.46 us (1%)
    pallas_call x1, Pallas kernels, body(): pl.pallas_call(functools.partial(kernel, lanes, wides, rate), out_shape=j...  101 us

profile of v6, /device:TPU:9, one launch (start us, length us, event | category | flops | bytes accessed | tf_op | source)
XLA Modules:
  0.0 102.7 jit_solution(9276848997561004383)
XLA Ops:
  0.7 0.0 copy-start
  0.7 0.8 copy-done
  1.5 100.6 %shard_map.46 = f32[64,256]{1,0:T(8,128)S(1)} custom-call(f32[64,256]{1,0:T(8,128)S(1)} %copy-done, bf16[512,512]{1,0:T(8,128)(2,1)} %x_ref.1, bf16[512,512]{1,0:T(8,128)(2,1)} %c_ref.1, s32[1,1]{1,0:T(1,128)S(6)} %copy.6.off_ref), custom_call_target="tpu_custom_call" | custom-call | flops 2415919104 | bytes 1048576 | tf_op jit(solution)/shard_map/pallas_call | solution.py:335
  102.1 0.6 copy.7
Async XLA Ops:
  0.7 0.8 copy-start
